TPU v7x, 256 devices: a whole 4x4x8 slice. The times are simulated.
256 devices in a mesh: group: 16 (over y_lo, z), fsdp: 16 (over x, y_hi, core).
Axes of the slice: x: 4, y: 4 (y_hi: 2, y_lo: 2; y = y_hi * 2 + y_lo), z: 8, core: 2. Of those that a mesh axis runs over, the one named last changes fastest.
Arguments:
- activations: bfloat16 [65536, 2560], P(('group', 'fsdp')), may hold values from -24 to 24
- cotangent: bfloat16 [65536, 2560], P(('group', 'fsdp')), may hold values from -6 to 6
- token_ids: int32 [65536], P(('group', 'fsdp')), may hold values from -100 to 31999, as said below
- step_count: int32 [1], replicated, may hold values from 0 to 7
- master: float32 [16, 2560, 2560], P('group', 'fsdp'), may hold values from -0.12 to 0.12
- first_moment: bfloat16 [16, 2560, 2560], P('group', 'fsdp'), may hold values from -150 to 150
- second_moment: bfloat16 [16, 2560, 2560], P('group', 'fsdp'), may hold values from 200 to 3200
Outputs:
- output: bfloat16 [65536, 2560], P(('group', 'fsdp'))
- act_grad: bfloat16 [65536, 2560], P(('group', 'fsdp'))
- new_master: float32 [16, 2560, 2560], P('group', 'fsdp')
- new_first: bfloat16 [16, 2560, 2560], P('group', 'fsdp')
- new_second: bfloat16 [16, 2560, 2560], P('group', 'fsdp')
Inputs may be any that keep to these rules, and one draw needn't show every extreme that they name: `token_ids`: token ids of a vocabulary of 32000, or -100 for tokens outside the loss; some token of every draw is -100 and some is 31999.
All inputs are finite; a program needn't handle non-finite values.
Results may differ from a plain program's by a relative error of at most 0.014.
Values may be sent and summed in bfloat16 or wider, within the bound.
No kernel may reach another device: no remote copies, remote signals or barrier semaphores. Data moves between devices by JAX's collectives and lax.ppermute only.
A program may use at most 128 MiB of HBM per device.

v0:
```python
from functools import partial

import jax
import jax.numpy as jnp
from jax import lax
from jax.experimental import pallas as pl
from jax.experimental.pallas import tpu as pltpu
from jax.sharding import PartitionSpec as P

beta_one = 0.9
beta_two = 0.95
learn_rate = 0.002
decay_rate = 0.1
epsilon = 1e-05

NX = 4
PIECE = 160
HALF = NX * PIECE

bf16 = jnp.bfloat16
f32 = jnp.float32
SMEM = pl.BlockSpec(memory_space=pltpu.SMEM)
VMEM = pl.BlockSpec(memory_space=pltpu.VMEM)
ANY = pl.BlockSpec(memory_space=pltpu.HBM)


def room(mebibytes):
    return pltpu.CompilerParams(vmem_limit_bytes=mebibytes * 1024 * 1024)


def along(move):
    pairs = []
    for f in range(16):
        x, h, c = move(f // 4, (f // 2) % 2, f % 2)
        pairs.append((f, (x % 4) * 4 + h * 2 + c))
    return pairs


NEXT = along(lambda x, h, c: (x + 1, h, c))
PREV = along(lambda x, h, c: (x - 1, h, c))
OPPOSITE = along(lambda x, h, c: (x + 2, h, c))
ACROSS = along(lambda x, h, c: (x, 1 - h, c))
DIAGONAL = along(lambda x, h, c: (x, 1 - h, 1 - c))
SIBLING = along(lambda x, h, c: (x, h, 1 - c))


def send(value, pairs):
    return lax.ppermute(value, "fsdp", pairs)


def cost(flops, moved):
    return pl.CostEstimate(flops=1, bytes_accessed=1, transcendentals=0)


def held_until(value, after):
    return pl.pallas_call(
        lambda *refs: None,
        out_shape=jax.ShapeDtypeStruct(value.shape, value.dtype),
        in_specs=[ANY] * (1 + len(after)),
        out_specs=ANY,
        input_output_aliases={0: 0},
        compiler_params=room(1),
        cost_estimate=cost(0, 0),
    )(value, *after)


def row_of(place, h, slot, j):
    x, c = place[0], place[2]
    core = c if slot == 0 else 1 - c
    return pl.multiple_of(lax.rem(x + j, NX) * (4 * PIECE) + h * (2 * PIECE) + core * PIECE, 32)


def prepare_kernel(place, act, cot, live, master, bias, mine, lead, own, shard, flipped, ordered):
    h = place[1]
    flipped[...] = act[...].T
    for slot in range(2):
        for j in range(NX):
            start = slot * HALF + j * PIECE
            ordered[pl.ds(start, PIECE), :] = flipped[pl.ds(row_of(place, 1 - h, slot, j), PIECE), :]
            start += 2 * HALF
            ordered[pl.ds(start, PIECE), :] = flipped[pl.ds(row_of(place, h, slot, j), PIECE), :]
    wide = cot.shape[1]
    lead[:, wide:] = ordered[: 2 * HALF, :].T
    own[...] = ordered[2 * HALF : 3 * HALF, :].T
    mine[:, wide:] = ordered[3 * HALF :, :].T
    masked = jnp.where(live[...] >= 0, cot[...], jnp.zeros((), bf16))
    lead[:, :wide] = masked
    mine[:, :wide] = masked
    shard[...] = master[...].astype(bf16)


def prepare(place, activations, cotangent, token_ids, master, bias):
    rows, wide = activations.shape
    shapes = [(rows, wide + HALF), (rows, wide + 2 * HALF), (rows, HALF), master.shape]
    return pl.pallas_call(
        prepare_kernel,
        out_shape=[jax.ShapeDtypeStruct(shape, bf16) for shape in shapes],
        in_specs=[SMEM, VMEM, VMEM, VMEM, VMEM, SMEM],
        out_specs=[VMEM] * 4,
        scratch_shapes=[pltpu.VMEM((wide, rows), bf16), pltpu.VMEM((wide, rows), bf16)],
        compiler_params=room(14),
        cost_estimate=cost(0, 8 * rows * wide),
    )(place, activations, cotangent, token_ids[:, None], master, bias)


OVER_ROWS = (((0,), (0,)), ((), ()))
OVER_COLUMNS = (((1,), (1,)), ((), ()))


def gradient_kernel(own, mine, beside, lead, diagonal, *refs):
    outs, flipped, gathered = refs[-2 * NX - 1 : -2], refs[-2], refs[-1]
    rows, wide = own.shape[0], outs[0].shape[1]
    acts = (own[...], beside[:, wide:], lead[:, wide : wide + HALF], diagonal[:, wide + HALF :])
    for i, act in enumerate(acts):
        flipped[:, i * rows : (i + 1) * rows] = act.T
    tile = gathered.shape[1]
    for k in range(wide // tile):
        cols = slice(k * tile, (k + 1) * tile)
        for i, grad in enumerate((mine, beside, lead, diagonal)):
            gathered[i * rows : (i + 1) * rows, :] = grad[:, cols]
        total = jnp.dot(flipped[...], gathered[...], preferred_element_type=f32)
        start = 0
        for out in outs:
            out[:, cols] = total[start : start + out.shape[0]].astype(out.dtype)
            start += out.shape[0]


def gradient_blocks(own, mine, beside, lead, diagonal, after):
    rows = own.shape[0]
    wide = mine.shape[1] - HALF
    return pl.pallas_call(
        gradient_kernel,
        out_shape=[jax.ShapeDtypeStruct((PIECE, wide), f32)]
        + [jax.ShapeDtypeStruct((PIECE // 2, wide), bf16)] * (2 * NX - 2),
        in_specs=[VMEM] * 5 + [ANY] * len(after),
        out_specs=[VMEM] * (2 * NX - 1),
        scratch_shapes=[pltpu.VMEM((HALF, 4 * rows), bf16), pltpu.VMEM((4 * rows, wide // 5), bf16)],
        compiler_params=room(10),
        cost_estimate=cost(8 * HALF * rows * wide, 10_000_000),
    )(own, mine, beside, lead, diagonal, *after)


def join_kernel(*refs):
    for left, right, out in zip(refs[0:2], refs[2:4], refs[4:6]):
        out[...] = (left[...].astype(f32) + right[...].astype(f32)).astype(bf16)


def join(ours, arrived):
    shape = ours[0].shape
    return pl.pallas_call(
        join_kernel,
        out_shape=[jax.ShapeDtypeStruct(shape, bf16)] * 2,
        in_specs=[VMEM] * 4,
        out_specs=[VMEM] * 2,
        compiler_params=room(6),
        cost_estimate=cost(2 * shape[0] * shape[1], 12 * shape[0] * shape[1]),
    )(*ours, *arrived)


def fetch(shards, gathered, sems):
    copies = []
    start = 0
    for i, shard in enumerate(shards):
        to = gathered.at[pl.ds(start, shard.shape[0]), :]
        copies.append(pltpu.make_async_copy(shard, to, sems.at[i]))
        start += shard.shape[0]
    for copy in copies:
        copy.start()
    for copy in copies:
        copy.wait()


def times_weights(flipped, gathered):
    return lax.dot_general(flipped, gathered, (((0,), (0,)), ((), ())), preferred_element_type=f32)


def output_kernel(count, lead, *refs):
    shards, (theirs, gathered) = refs[:count], refs[-2:]
    for i, shard in enumerate(shards):
        gathered[i * PIECE : (i + 1) * PIECE, :] = shard[...]
    theirs[...] = jnp.dot(lead[...], gathered[...], preferred_element_type=f32).astype(bf16)


def output_part(lead, weights, after):
    depth = 2 * HALF
    rows = lead.shape[0]
    wide = weights[0].shape[1]
    steps = 5
    tile = wide // steps
    return pl.pallas_call(
        partial(output_kernel, len(weights)),
        grid=(steps,),
        out_shape=jax.ShapeDtypeStruct((rows, wide), bf16),
        in_specs=[pl.BlockSpec((rows, depth), lambda i: (0, wide // depth))]
        + [pl.BlockSpec((PIECE, tile), lambda i: (0, i))] * len(weights)
        + [ANY] * len(after),
        out_specs=pl.BlockSpec((rows, tile), lambda i: (0, i)),
        scratch_shapes=[pltpu.VMEM((depth, tile), bf16)],
        compiler_params=room(12),
        cost_estimate=cost(2 * depth * rows * wide, 2 * depth * wide + 4 * rows * wide),
    )(lead, *weights, *after)


def products_kernel(count, mine, lead, own, *refs):
    shards = refs[:count]
    theirs, ours, base, gathered, sems = refs[-5:]
    fetch(shards, gathered, sems)
    wide = base.shape[1]
    for out, grad in ((theirs, lead), (ours, mine)):
        back = lax.dot_general(gathered[...], grad[:, :wide], OVER_COLUMNS, preferred_element_type=f32)
        out[...] = back.astype(bf16)
    total = jnp.dot(own[...], gathered[:HALF, :], preferred_element_type=f32)
    base[...] = total + jnp.dot(mine[:, wide:], gathered[HALF:, :], preferred_element_type=f32)


def products(mine, lead, own, weights, after):
    depth = 2 * HALF
    rows = own.shape[0]
    wide = weights[0].shape[1]
    return pl.pallas_call(
        partial(products_kernel, len(weights)),
        out_shape=[jax.ShapeDtypeStruct((depth, rows), bf16)] * 2 + [jax.ShapeDtypeStruct((rows, wide), f32)],
        in_specs=[VMEM] * 3 + [ANY] * (len(weights) + len(after)),
        out_specs=[VMEM] * 3,
        scratch_shapes=[pltpu.VMEM((depth, wide), bf16), pltpu.SemaphoreType.DMA((len(weights),))],
        compiler_params=room(16),
        cost_estimate=cost(6 * depth * rows * wide, 2 * depth * wide + 10 * rows * wide),
    )(mine, lead, own, *weights, *after)


def adam_kernel(bias, master, first, second, here, *refs):
    low, high = refs[0:2], refs[2:4]
    stepped, sent, first_out, second_out = refs[-4:]

    def update(arrived):
        gradient = here[...]
        for part in arrived:
            gradient += part[...].astype(f32)
        rows = master[...]
        first_new = beta_one * first[...].astype(f32) + (1.0 - beta_one) * gradient
        second_new = beta_two * second[...].astype(f32) + (1.0 - beta_two) * gradient * gradient
        first_hat = first_new / bias[0]
        second_hat = second_new / bias[1]
        delta = learn_rate * (first_hat / (jnp.sqrt(second_hat) + epsilon) + decay_rate * rows)
        stepped[...] = rows - delta
        sent[...] = (rows - delta).astype(bf16)
        first_out[...] = first_new.astype(bf16)
        second_out[...] = second_new.astype(bf16)

    first_half = pl.program_id(0) < pl.num_programs(0) // 2

    @pl.when(first_half)
    def _():
        update(low)

    @pl.when(jnp.logical_not(first_half))
    def _():
        update(high)


def adam(bias, master, first, second, here, low, high):
    rows, wide = master.shape
    steps = 2
    turn = steps // 2
    part = pl.BlockSpec((rows // steps, wide), lambda i: (i, 0))
    lows = pl.BlockSpec((rows // steps, wide), lambda i: (jnp.minimum(i, turn - 1), 0))
    highs = pl.BlockSpec((rows // steps, wide), lambda i: (jnp.maximum(i - turn, 0), 0))
    return pl.pallas_call(
        adam_kernel,
        grid=(steps,),
        out_shape=[jax.ShapeDtypeStruct((rows, wide), f32)] + [jax.ShapeDtypeStruct((rows, wide), bf16)] * 3,
        in_specs=[SMEM] + [part] * 4 + [lows] * 2 + [highs] * 2,
        out_specs=[part] * 4,
        compiler_params=room(18),
        cost_estimate=cost(20 * rows * wide, 26 * rows * wide),
    )(bias, master, first, second, here, *low, *high)


def finish_kernel(place, ours, theirs, base, arrived, stepped, other, output, act_grad, averaged, ordered):
    h = place[1]
    step = pl.program_id(0)

    @pl.when(step == 0)
    def _():
        for slot in range(2):
            for j in range(NX):
                start = slot * HALF + j * PIECE
                piece = slice(start, start + PIECE)
                ordered[pl.ds(row_of(place, h, slot, j), PIECE), :] = ours[piece, :]
                ordered[pl.ds(row_of(place, 1 - h, slot, j), PIECE), :] = theirs[piece, :]

    width = act_grad.shape[1]
    act_grad[...] = ordered[pl.ds(pl.multiple_of(step * width, width), width), :].T
    output[...] = (base[...] + arrived[...].astype(f32)).astype(bf16)
    averaged[...] = 0.5 * (stepped[...] + other[...].astype(f32))


def finish(place, ours, theirs, base, arrived, stepped, other):
    rows, wide = base.shape
    depth = ours.shape[0]
    mine = stepped.shape[0]
    steps = 5
    cols = pl.BlockSpec((rows, wide // steps), lambda i: (0, i))
    part = pl.BlockSpec((mine // steps, wide), lambda i: (i, 0))
    whole = pl.BlockSpec((depth, rows), lambda i: (0, 0))
    return pl.pallas_call(
        finish_kernel,
        grid=(steps,),
        out_shape=[
            jax.ShapeDtypeStruct((rows, wide), bf16),
            jax.ShapeDtypeStruct((rows, 2 * depth), bf16),
            jax.ShapeDtypeStruct((mine, wide), f32),
        ],
        in_specs=[SMEM, whole, whole, cols, cols, part, part],
        out_specs=[cols, cols, part],
        scratch_shapes=[pltpu.VMEM((2 * depth, rows), bf16)],
        compiler_params=room(14),
        cost_estimate=cost(4 * rows * wide, 18 * rows * wide),
    )(place, ours, theirs, base, arrived, stepped, other)


def from_partner(value, bit_index):
    mask = 2**bit_index
    pairs = [(source, source ^ mask) for source in range(lax.axis_size("group"))]
    return lax.ppermute(value, "group", pairs)


def exchange(sent, beside, bit_index):
    levels = lax.axis_size("group").bit_length() - 1

    def branch(level, value, rest):
        return from_partner(value, level), [send(part, pairs) for part, pairs in zip(rest, moves)]

    rest, moves = [part for part, _ in beside], [pairs for _, pairs in beside]
    return lax.switch(bit_index, [partial(branch, level) for level in range(levels)], sent, rest)


def shards(activations, cotangent, token_ids, step_count, master, first_moment, second_moment):
    master, first_old, second_old = master[0], first_moment[0], second_moment[0]
    levels = lax.axis_size("group").bit_length() - 1
    bit_index = step_count[0] % levels
    f = lax.axis_index("fsdp")
    place = jnp.stack([f // 4, (f // 2) % 2, f % 2]).astype(jnp.int32)
    steps_done = (step_count[0] + 1).astype(f32)
    bias = jnp.stack([1.0 - jnp.power(f32(beta_one), steps_done), 1.0 - jnp.power(f32(beta_two), steps_done)])

    mine, lead, own, shard = prepare(place, activations, cotangent, token_ids, master, bias)
    lead, beside = send(lead, ACROSS), send(mine, SIBLING)
    pieces = [shard, send(shard, PREV), send(shard, OPPOSITE), send(shard, NEXT)]
    weights = pieces + [send(part, SIBLING) for part in pieces]
    lead = held_until(lead, [*weights[NX:], beside])
    output = output_part(lead, weights, [])
    blocks = gradient_blocks(own, mine, beside, lead, send(lead, SIBLING), [output])
    output = send(output, ACROSS)
    here, next_low, next_high, far_low, far_high, prev_low, prev_high = blocks
    next_low, prev_high = join((next_low, prev_high), (send(far_low, NEXT), send(far_high, PREV)))
    low = [send(next_low, NEXT), send(prev_low, PREV)]
    high = [send(next_high, NEXT), send(prev_high, PREV)]
    theirs, ours, base = products(mine, lead, own, weights, [next_low])
    stepped, sent, first_out, second_out = adam(bias, master, first_old, second_old, here, low, high)
    arrived, (theirs,) = exchange(sent, [(theirs, ACROSS)], bit_index)
    output, act_grad, averaged = finish(place, ours, theirs, base, output, stepped, arrived)
    return (output, act_grad, averaged[None], first_out[None], second_out[None])


def solution(mesh):
    rows = P(("group", "fsdp"), None)
    state = P("group", "fsdp", None)
    return jax.shard_map(
        shards,
        mesh=mesh,
        in_specs=(rows, rows, P(("group", "fsdp")), P(), state, state, state),
        out_specs=(rows, rows, state, state, state),
        check_vma=False,
    )
```

profile of v0, /device:TPU:1, one launch (start us, length us, event | category | flops | bytes accessed | tf_op | source)
XLA Modules:
  0.0 152.4 jit_solution(15998357368573277545)
XLA Ops:
  2.4 1.4 copy-done.6
  3.8 1.3 copy-done.22
  5.2 1.3 copy-done.23
  6.5 1.6 %shard_map.110 = (bf16[256,3200]{1,0:T(8,128)(2,1)S(1)}, bf16[256,3840]{1,0:T(8,128)(2,1)S(1)}, bf16[256,640]{1,0:T(8,128)(2,1)S(1)}, bf16[160,2560]{1,0:T(8,128)(2,1)S(1)}) custom-call(s32[3]{0:T(128)S(1)} %pad_add_fusion.place, bf16[256,2560]{1,0:T(8,128)(2,1)S(1)} %copy-done.22, bf16[256,2560]{1,0:T(8,128)(2,1)S(1)} %copy-done.23, ...), custom_call_target="tpu_custom_call" | custom-call | flops 1 | bytes 1 | tf_op jit(solution)/shard_map/pallas_call | solution.py:95
  8.1 3.3 %collective-permute-start.9 = (bf16[160,2560]{1,0:T(8,128)(2,1)S(1)}, bf16[160,2560]{1,0:T(8,128)(2,1)S(1)}, u32[]{:S(2)}, u32[]{:S(2)}) collective-permute-start(bf16[160,2560]{1,0:T(8,128)(2,1)S(1)} %get-tuple-element.56.refs_0_), channel_id=1, source_target_pairs={{0,1},{1,0},{2,3},{3,2},{4,5},{5,4},{6,7},{7,6},{8,9},{9,8},{10,11... | collective-permute-start | bytes 2457608 | tf_op jit(solution)/shard_map/ppermute | solution.py:48
  12.6 2.5 %collective-permute-start.10 = (bf16[160,2560]{1,0:T(8,128)(2,1)S(1)}, bf16[160,2560]{1,0:T(8,128)(2,1)S(1)}, u32[]{:S(2)}, u32[]{:S(2)}) collective-permute-start(bf16[160,2560]{1,0:T(8,128)(2,1)S(1)} %get-tuple-element.56.refs_0_), channel_id=1, source_target_pairs={{0,12},{1,13},{2,14},{3,15},{4,0},{5,1},{6,2},{7,3},{8,4},{9,5},{1... | collective-permute-start | bytes 2457608 | tf_op jit(solution)/shard_map/ppermute | solution.py:48
  17.4 32.3 %collective-permute-done.10.refs_1_ = bf16[160,2560]{1,0:T(8,128)(2,1)S(1)} collective-permute-done((bf16[160,2560]{1,0:T(8,128)(2,1)S(1)}, bf16[160,2560]{1,0:T(8,128)(2,1)S(1)}, u32[]{:S(2)}, u32[]{:S(2)}) %collective-permute-start.10) | collective-permute-done | bytes 819232 | tf_op jit(solution)/shard_map/ppermute | solution.py:48
  49.8 1.4 collective-permute-start.11
  51.2 3.1 %collective-permute-done.14.refs_3_ = bf16[160,2560]{1,0:T(8,128)(2,1)S(1)} collective-permute-done((bf16[160,2560]{1,0:T(8,128)(2,1)S(1)}, bf16[160,2560]{1,0:T(8,128)(2,1)S(1)}, u32[]{:S(2)}, u32[]{:S(2)}) %collective-permute-start.14) | collective-permute-done | bytes 819232 | tf_op jit(solution)/shard_map/ppermute | solution.py:48
  54.8 1.9 %collective-permute-done.15.refs_4_.refs_7_ = bf16[160,2560]{1,0:T(8,128)(2,1)S(1)} collective-permute-done((bf16[160,2560]{1,0:T(8,128)(2,1)S(1)}, bf16[160,2560]{1,0:T(8,128)(2,1)S(1)}, u32[]{:S(2)}, u32[]{:S(2)}) %collective-permute-start.15) | collective-permute-done | bytes 819232 | tf_op jit(solution)/shard_map/ppermute | solution.py:48
  58.2 4.0 %shard_map.112.refs_0_ = bf16[256,2560]{1,0:T(8,128)(2,1)} custom-call(bf16[256,3840]{1,0:T(8,128)(2,1)S(1)} %shard_map.111.lead, bf16[160,2560]{1,0:T(8,128)(2,1)S(1)} %get-tuple-element.56.refs_0_, bf16[160,2560]{1,0:T(8,128)(2,1)S(1)} %collective-permute-done.10.refs_1_, bf16[160,2560]{1,0:T(8,128)(2,1)S(1)} %collective-permute-done.12.refs_2_, ...), custom_call_target="tpu_custom_call" | custom-call | flops 1 | bytes 1 | tf_op jit(solution)/shard_map/pallas_call | solution.py:190
  63.4 4.4 %shard_map.113 = (f32[160,2560]{1,0:T(8,128)S(1)}, bf16[80,2560]{1,0:T(8,128)(2,1)S(1)}, bf16[80,2560]{1,0:T(8,128)(2,1)}, bf16[80,2560]{1,0:T(8,128)(2,1)S(1)},...) custom-call(bf16[256,640]{1,0:T(8,128)(2,1)S(1)} %get-tuple-element.57.own, ...), custom_call_target="tpu_custom_call" | custom-call | flops 1 | bytes 1 | tf_op jit(solution)/shard_map/pallas_call | solution.py:131
  70.3 1.5 collective-permute-start.19
  73.2 7.9 %collective-permute-done.18.refs_2_ = bf16[80,2560]{1,0:T(8,128)(2,1)S(1)} collective-permute-done((bf16[80,2560]{1,0:T(8,128)(2,1)S(1)}, bf16[80,2560]{1,0:T(8,128)(2,1)S(1)}, u32[]{:S(2)}, u32[]{:S(2)}) %collective-permute-start.18) | collective-permute-done | bytes 409632 | tf_op jit(solution)/shard_map/ppermute | solution.py:48
  83.1 1.8 %collective-permute-start.23 = (bf16[80,2560]{1,0:T(8,128)(2,1)}, bf16[80,2560]{1,0:T(8,128)(2,1)}, u32[]{:S(2)}, u32[]{:S(2)}) collective-permute-start(bf16[80,2560]{1,0:T(8,128)(2,1)} %get-tuple-element.67), channel_id=1, source_target_pairs={{0,12},{1,13},{2,14},{3,15},{4,0},{5,1},{6,2},{7,3},{8,4},{9,5},{1... | collective-permute-start | bytes 1228808 | tf_op jit(solution)/shard_map/ppermute | solution.py:48
  88.3 1.4 copy-done.9
  94.3 6.5 %shard_map.115 = (bf16[1280,256]{1,0:T(8,128)(2,1)S(1)}, bf16[1280,256]{1,0:T(8,128)(2,1)S(1)}, f32[256,2560]{1,0:T(8,128)S(1)}) custom-call(bf16[256,3200]{1,0:T(8,128)(2,1)S(1)} %copy-done.9, bf16[256,3840]{1,0:T(8,128)(2,1)S(1)} %shard_map.111.lead, bf16[256,640]{1,0:T(8,128)(2,1)S(1)} %get-tuple-element.57.own, bf16[160,2560]{1,0:T(8,128)(2,1)S(1)} %copy-done.11, ...), custom_call_target="tpu_custom_call" | custom-call | flops 1 | bytes 1 | tf_op jit(solution)/shard_map/pallas_call | solution.py:220
  100.9 4.9 %shard_map.116 = (f32[160,2560]{1,0:T(8,128)S(1)}, bf16[160,2560]{1,0:T(8,128)(2,1)S(1)}, bf16[160,2560]{1,0:T(8,128)(2,1)}, bf16[160,2560]{1,0:T(8,128)(2,1)}) custom-call(f32[2]{0:T(128)S(1)} %pad_maximum_fusion.bias, f32[160,2560]{1,0:T(8,128)S(1)} %bitcast.18, bf16[160,2560]{1,0:T(8,128)(2,1)S(1)} %bitcast.19, bf16[160,2560]{1,0:T(8,128)(2,1)S(1)} %bitcast.20, ...), custom_call_target="tpu_custom_call" | custom-call | flops 1 | bytes 1 | tf_op jit(solution)/shard_map/pallas_call | solution.py:268
  105.9 38.0 %conditional.1 = (bf16[160,2560]{1,0:T(8,128)(2,1)}, bf16[1280,256]{1,0:T(8,128)(2,1)}) conditional(s32[]{:T(128)} %clamp.3, (bf16[160,2560]{1,0:T(8,128)(2,1)S(1)}, bf16[1280,256]{1,0:T(8,128)(2,1)S(1)}) %tuple.24, (bf16[160,2560]{1,0:T(8,128)(2,1)S(1)}, bf16[1280,256]{1,0:T(8,128)(2,1)S(1)}) %tuple.24, ...), branch_computations={%region_0.1_spmd, %region_1.2_spmd, %region_2.3_spmd, %region_3.4_... | conditional | bytes 5898336 | solution.py:335
  105.9 3.1 %collective-permute-start.2 = (bf16[160,2560]{1,0:T(8,128)(2,1)S(1)}, bf16[160,2560]{1,0:T(8,128)(2,1)}, u32[]{:S(2)}, u32[]{:S(2)}) collective-permute-start(bf16[160,2560]{1,0:T(8,128)(2,1)S(1)} %get-tuple-element.18), channel_id=1, source_target_pairs={{0,32},{16,48},{32,0},{48,16},{64,96},{80,112},{96,64},{112,80},{1... | collective-permute-start | bytes 2457608 | tf_op jit(solution)/shard_map/cond/branch_1_fun/ppermute | solution.py:325
  109.7 14.2 %collective-permute-done.3 = bf16[1280,256]{1,0:T(8,128)(2,1)} collective-permute-done((bf16[1280,256]{1,0:T(8,128)(2,1)S(1)}, bf16[1280,256]{1,0:T(8,128)(2,1)}, u32[]{:S(2)}, u32[]{:S(2)}) %collective-permute-start.3) | collective-permute-done | bytes 655392 | tf_op jit(solution)/shard_map/cond/branch_1_fun/ppermute | solution.py:48
  123.9 20.0 %collective-permute-done.2 = bf16[160,2560]{1,0:T(8,128)(2,1)} collective-permute-done((bf16[160,2560]{1,0:T(8,128)(2,1)S(1)}, bf16[160,2560]{1,0:T(8,128)(2,1)}, u32[]{:S(2)}, u32[]{:S(2)}) %collective-permute-start.2) | collective-permute-done | bytes 819232 | tf_op jit(solution)/shard_map/cond/branch_1_fun/ppermute | solution.py:325
  143.9 1.7 %copy-done.19 = f32[256,2560]{1,0:T(8,128)S(1)} copy-done((f32[256,2560]{1,0:T(8,128)S(1)}, f32[256,2560]{1,0:T(8,128)}, u32[]{:S(2)}) %copy-start.19) | copy-done | bytes 2621464
  146.7 5.7 %shard_map.117 = (bf16[256,2560]{1,0:T(8,128)(2,1)}, bf16[256,2560]{1,0:T(8,128)(2,1)}, f32[160,2560]{1,0:T(8,128)}) custom-call(s32[3]{0:T(128)S(1)} %pad_add_fusion.place, bf16[1280,256]{1,0:T(8,128)(2,1)S(1)} %copy-done.27, bf16[1280,256]{1,0:T(8,128)(2,1)} %get-tuple-element.70.theirs, f32[256,2560]{1,0:T(8,128)S(1)} %copy-done.19, ...), custom_call_target="tpu_custom_call" | custom-call | flops 1 | bytes 1 | tf_op jit(solution)/shard_map/pallas_call | solution.py:306
  (82 shorter events, 23.4 us)
Async XLA Ops:
  8.1 50.1 %copy-start.10 = (bf16[160,2560]{1,0:T(8,128)(2,1)}, bf16[160,2560]{1,0:T(8,128)(2,1)S(1)}, u32[]{:S(2)}) copy-start(bf16[160,2560]{1,0:T(8,128)(2,1)S(1)} %get-tuple-element.56.refs_0_) | copy-start | bytes 2457604
  8.1 55.3 %copy-start.8 = (bf16[256,3200]{1,0:T(8,128)(2,1)}, bf16[256,3200]{1,0:T(8,128)(2,1)S(1)}, u32[]{:S(2)}) copy-start(bf16[256,3200]{1,0:T(8,128)(2,1)S(1)} %get-tuple-element.54.mine) | copy-start | bytes 4915204
  8.1 8.1 %collective-permute-start.9 = (bf16[160,2560]{1,0:T(8,128)(2,1)S(1)}, bf16[160,2560]{1,0:T(8,128)(2,1)S(1)}, u32[]{:S(2)}, u32[]{:S(2)}) collective-permute-start(bf16[160,2560]{1,0:T(8,128)(2,1)S(1)} %get-tuple-element.56.refs_0_), channel_id=1, source_target_pairs={{0,1},{1,0},{2,3},{3,2},{4,5},{5,4},{6,7},{7,6},{8,9},{9,8},{10,11... | collective-permute-start | bytes 2457608 | tf_op jit(solution)/shard_map/ppermute | solution.py:48
  11.4 45.9 %collective-permute-start.8 = (bf16[256,3840]{1,0:T(8,128)(2,1)S(1)}, bf16[256,3840]{1,0:T(8,128)(2,1)S(1)}, u32[]{:S(2)}, u32[]{:S(2)}) collective-permute-start(bf16[256,3840]{1,0:T(8,128)(2,1)S(1)} %get-tuple-element.55), channel_id=1, source_target_pairs={{0,2},{1,3},{2,0},{3,1},{4,6},{5,7},{6,4},{7,5},{8,10},{9,11},{10,... | collective-permute-start | bytes 5898248 | tf_op jit(solution)/shard_map/ppermute | solution.py:48
  12.6 37.2 %collective-permute-start.10 = (bf16[160,2560]{1,0:T(8,128)(2,1)S(1)}, bf16[160,2560]{1,0:T(8,128)(2,1)S(1)}, u32[]{:S(2)}, u32[]{:S(2)}) collective-permute-start(bf16[160,2560]{1,0:T(8,128)(2,1)S(1)} %get-tuple-element.56.refs_0_), channel_id=1, source_target_pairs={{0,12},{1,13},{2,14},{3,15},{4,0},{5,1},{6,2},{7,3},{8,4},{9,5},{1... | collective-permute-start | bytes 2457608 | tf_op jit(solution)/shard_map/ppermute | solution.py:48
  15.1 36.1 %collective-permute-start.12 = (bf16[160,2560]{1,0:T(8,128)(2,1)S(1)}, bf16[160,2560]{1,0:T(8,128)(2,1)S(1)}, u32[]{:S(2)}, u32[]{:S(2)}) collective-permute-start(bf16[160,2560]{1,0:T(8,128)(2,1)S(1)} %get-tuple-element.56.refs_0_), channel_id=1, source_target_pairs={{0,8},{1,9},{2,10},{3,11},{4,12},{5,13},{6,14},{7,15},{8,0},{9,1},... | collective-permute-start | bytes 2457608 | tf_op jit(solution)/shard_map/ppermute | solution.py:48
  15.6 38.7 %collective-permute-start.14 = (bf16[160,2560]{1,0:T(8,128)(2,1)S(1)}, bf16[160,2560]{1,0:T(8,128)(2,1)S(1)}, u32[]{:S(2)}, u32[]{:S(2)}) collective-permute-start(bf16[160,2560]{1,0:T(8,128)(2,1)S(1)} %get-tuple-element.56.refs_0_), channel_id=1, source_target_pairs={{0,4},{1,5},{2,6},{3,7},{4,8},{5,9},{6,10},{7,11},{8,12},{9,13},{1... | collective-permute-start | bytes 2457608 | tf_op jit(solution)/shard_map/ppermute | solution.py:48
  16.2 40.6 %collective-permute-start.16 = (bf16[256,3200]{1,0:T(8,128)(2,1)S(1)}, bf16[256,3200]{1,0:T(8,128)(2,1)S(1)}, u32[]{:S(2)}, u32[]{:S(2)}) collective-permute-start(bf16[256,3200]{1,0:T(8,128)(2,1)S(1)} %get-tuple-element.54.mine), channel_id=1, source_target_pairs={{0,1},{1,0},{2,3},{3,2},{4,5},{5,4},{6,7},{7,6},{8,9},{9,8},{10,11... | collective-permute-start | bytes 4915208 | tf_op jit(solution)/shard_map/ppermute | solution.py:48
  49.8 8.4 %copy-start.12 = (bf16[160,2560]{1,0:T(8,128)(2,1)}, bf16[160,2560]{1,0:T(8,128)(2,1)S(1)}, u32[]{:S(2)}) copy-start(bf16[160,2560]{1,0:T(8,128)(2,1)S(1)} %collective-permute-done.10.refs_1_) | copy-start | bytes 2457604
  49.8 5.0 %collective-permute-start.11 = (bf16[160,2560]{1,0:T(8,128)(2,1)S(1)}, bf16[160,2560]{1,0:T(8,128)(2,1)S(1)}, u32[]{:S(2)}, u32[]{:S(2)}) collective-permute-start(bf16[160,2560]{1,0:T(8,128)(2,1)S(1)} %collective-permute-done.10.refs_1_), channel_id=1, source_target_pairs={{0,1},{1,0},{2,3},{3,2},{4,5},{5,4},{6,7},{7,6},{8,9},{9,8},{10,11... | collective-permute-start | bytes 2457608 | tf_op jit(solution)/shard_map/ppermute | solution.py:48
  51.1 7.0 %copy-start.14 = (bf16[160,2560]{1,0:T(8,128)(2,1)}, bf16[160,2560]{1,0:T(8,128)(2,1)S(1)}, u32[]{:S(2)}) copy-start(bf16[160,2560]{1,0:T(8,128)(2,1)S(1)} %collective-permute-done.12.refs_2_) | copy-start | bytes 2457604
  51.1 3.7 %collective-permute-start.13 = (bf16[160,2560]{1,0:T(8,128)(2,1)S(1)}, bf16[160,2560]{1,0:T(8,128)(2,1)S(1)}, u32[]{:S(2)}, u32[]{:S(2)}) collective-permute-start(bf16[160,2560]{1,0:T(8,128)(2,1)S(1)} %collective-permute-done.12.refs_2_), channel_id=1, source_target_pairs={{0,1},{1,0},{2,3},{3,2},{4,5},{5,4},{6,7},{7,6},{8,9},{9,8},{10,11... | collective-permute-start | bytes 2457608 | tf_op jit(solution)/shard_map/ppermute | solution.py:48
  54.3 2.5 %collective-permute-start.15 = (bf16[160,2560]{1,0:T(8,128)(2,1)S(1)}, bf16[160,2560]{1,0:T(8,128)(2,1)S(1)}, u32[]{:S(2)}, u32[]{:S(2)}) collective-permute-start(bf16[160,2560]{1,0:T(8,128)(2,1)S(1)} %collective-permute-done.14.refs_3_), channel_id=1, source_target_pairs={{0,1},{1,0},{2,3},{3,2},{4,5},{5,4},{6,7},{7,6},{8,9},{9,8},{10,11... | collective-permute-start | bytes 2457608 | tf_op jit(solution)/shard_map/ppermute | solution.py:48
  57.3 6.1 %collective-permute-start.17 = (bf16[256,3840]{1,0:T(8,128)(2,1)S(1)}, bf16[256,3840]{1,0:T(8,128)(2,1)S(1)}, u32[]{:S(2)}, u32[]{:S(2)}) collective-permute-start(bf16[256,3840]{1,0:T(8,128)(2,1)S(1)} %shard_map.111.lead), channel_id=1, source_target_pairs={{0,1},{1,0},{2,3},{3,2},{4,5},{5,4},{6,7},{7,6},{8,9},{9,8},{10,11... | collective-permute-start | bytes 5898248 | tf_op jit(solution)/shard_map/ppermute | solution.py:48
  62.2 81.7 %collective-permute-start.24 = (bf16[256,2560]{1,0:T(8,128)(2,1)}, bf16[256,2560]{1,0:T(8,128)(2,1)}, u32[]{:S(2)}, u32[]{:S(2)}) collective-permute-start(bf16[256,2560]{1,0:T(8,128)(2,1)} %shard_map.112.refs_0_), channel_id=1, source_target_pairs={{0,2},{1,3},{2,0},{3,1},{4,6},{5,7},{6,4},{7,5},{8,10},{9,11},{10,... | collective-permute-start | bytes 3932168 | tf_op jit(solution)/shard_map/ppermute | solution.py:48
  69.1 12.1 %collective-permute-start.18 = (bf16[80,2560]{1,0:T(8,128)(2,1)S(1)}, bf16[80,2560]{1,0:T(8,128)(2,1)S(1)}, u32[]{:S(2)}, u32[]{:S(2)}) collective-permute-start(bf16[80,2560]{1,0:T(8,128)(2,1)S(1)} %get-tuple-element.60), channel_id=1, source_target_pairs={{0,4},{1,5},{2,6},{3,7},{4,8},{5,9},{6,10},{7,11},{8,12},{9,13},{1... | collective-permute-start | bytes 1228808 | tf_op jit(solution)/shard_map/ppermute | solution.py:48
  70.3 10.9 %collective-permute-start.19 = (bf16[80,2560]{1,0:T(8,128)(2,1)S(1)}, bf16[80,2560]{1,0:T(8,128)(2,1)S(1)}, u32[]{:S(2)}, u32[]{:S(2)}) collective-permute-start(bf16[80,2560]{1,0:T(8,128)(2,1)S(1)} %get-tuple-element.61), channel_id=1, source_target_pairs={{0,12},{1,13},{2,14},{3,15},{4,0},{5,1},{6,2},{7,3},{8,4},{9,5},{1... | collective-permute-start | bytes 1228808 | tf_op jit(solution)/shard_map/ppermute | solution.py:48
  71.7 29.1 %collective-permute-start.21 = (bf16[80,2560]{1,0:T(8,128)(2,1)}, bf16[80,2560]{1,0:T(8,128)(2,1)S(1)}, u32[]{:S(2)}, u32[]{:S(2)}) collective-permute-start(bf16[80,2560]{1,0:T(8,128)(2,1)} %get-tuple-element.65), channel_id=1, source_target_pairs={{0,12},{1,13},{2,14},{3,15},{4,0},{5,1},{6,2},{7,3},{8,4},{9,5},{1... | collective-permute-start | bytes 1228808 | tf_op jit(solution)/shard_map/ppermute | solution.py:48
  73.0 27.8 %collective-permute-start.22 = (bf16[80,2560]{1,0:T(8,128)(2,1)}, bf16[80,2560]{1,0:T(8,128)(2,1)}, u32[]{:S(2)}, u32[]{:S(2)}) collective-permute-start(bf16[80,2560]{1,0:T(8,128)(2,1)} %get-tuple-element.66), channel_id=1, source_target_pairs={{0,4},{1,5},{2,6},{3,7},{4,8},{5,9},{6,10},{7,11},{8,12},{9,13},{1... | collective-permute-start | bytes 1228808 | tf_op jit(solution)/shard_map/ppermute | solution.py:48
  82.2 18.7 %collective-permute-start.20 = (bf16[80,2560]{1,0:T(8,128)(2,1)}, bf16[80,2560]{1,0:T(8,128)(2,1)}, u32[]{:S(2)}, u32[]{:S(2)}) collective-permute-start(bf16[80,2560]{1,0:T(8,128)(2,1)} %get-tuple-element.62.refs_8_), channel_id=1, source_target_pairs={{0,4},{1,5},{2,6},{3,7},{4,8},{5,9},{6,10},{7,11},{8,12},{9,13},{1... | collective-permute-start | bytes 1228808 | tf_op jit(solution)/shard_map/ppermute | solution.py:48
  83.1 17.8 %collective-permute-start.23 = (bf16[80,2560]{1,0:T(8,128)(2,1)}, bf16[80,2560]{1,0:T(8,128)(2,1)}, u32[]{:S(2)}, u32[]{:S(2)}) collective-permute-start(bf16[80,2560]{1,0:T(8,128)(2,1)} %get-tuple-element.67), channel_id=1, source_target_pairs={{0,12},{1,13},{2,14},{3,15},{4,0},{5,1},{6,2},{7,3},{8,4},{9,5},{1... | collective-permute-start | bytes 1228808 | tf_op jit(solution)/shard_map/ppermute | solution.py:48
  94.3 6.6 %copy-start.25 = (bf16[1,160,2560]{2,1,0:T(8,128)(2,1)S(1)}, bf16[1,160,2560]{2,1,0:T(8,128)(2,1)}, u32[]{:S(2)}) copy-start(bf16[1,160,2560]{2,1,0:T(8,128)(2,1)} %param.17) | copy-start | bytes 2457604
  105.9 38.0 %collective-permute-start.2 = (bf16[160,2560]{1,0:T(8,128)(2,1)S(1)}, bf16[160,2560]{1,0:T(8,128)(2,1)}, u32[]{:S(2)}, u32[]{:S(2)}) collective-permute-start(bf16[160,2560]{1,0:T(8,128)(2,1)S(1)} %get-tuple-element.18), channel_id=1, source_target_pairs={{0,32},{16,48},{32,0},{48,16},{64,96},{80,112},{96,64},{112,80},{1... | collective-permute-start | bytes 2457608 | tf_op jit(solution)/shard_map/cond/branch_1_fun/ppermute | solution.py:325
  108.9 14.9 %collective-permute-start.3 = (bf16[1280,256]{1,0:T(8,128)(2,1)S(1)}, bf16[1280,256]{1,0:T(8,128)(2,1)}, u32[]{:S(2)}, u32[]{:S(2)}) collective-permute-start(bf16[1280,256]{1,0:T(8,128)(2,1)S(1)} %get-tuple-element.19), channel_id=1, source_target_pairs={{0,2},{1,3},{2,0},{3,1},{4,6},{5,7},{6,4},{7,5},{8,10},{9,11},{10,... | collective-permute-start | bytes 1966088 | tf_op jit(solution)/shard_map/cond/branch_1_fun/ppermute | solution.py:48
  (23 other events, 59.4 us)
where the time goes:
time: 151 us; the launch traced here: 152 us
  waiting for transfers between devices  80.1 us (53%)
  Pallas kernels  28.2 us (19%)
  starting transfers between devices  24 us (16%)
  local copies, waits for them, and re-layouts  18.4 us (12%)
  between operations  1.64 us (1%)
    ppermute x18, waiting for transfers between devices, send(): return lax.ppermute(value, 'fsdp', pairs)  60.1 us
    ppermute x18, starting transfers between devices, send(): return lax.ppermute(value, 'fsdp', pairs)  20.9 us
    ppermute x1, waiting for transfers between devices, from_partner(): return lax.ppermute(value, 'group', pairs)  20 us
    unnamed x56, local copies, waits for them, and re-layouts  17.6 us
    pallas_call x1, Pallas kernels, products(): pl.pallas_call(partial(products_kernel, len(weights)), out_shape=[jax.Sha...  6.48 us
    pallas_call x1, Pallas kernels, finish(): pl.pallas_call(finish_kernel, grid=(steps,), out_shape=[jax.ShapeDtypeStr...  5.66 us
    pallas_call x1, Pallas kernels, adam(): pl.pallas_call(adam_kernel, grid=(steps,), out_shape=[jax.ShapeDtypeStruc...  4.95 us
    pallas_call x1, Pallas kernels, gradient_blocks(): pl.pallas_call(gradient_kernel, out_shape=[jax.ShapeDtypeStruct((PIECE, w...  4.45 us
  transfers between devices with their start and end apart: 19, of which 7 were waited for; matrix products, arithmetic and copies ran while one was open for 0% of the time, Pallas kernels for 14%

commit v1 on v0

--- a/solution.py
+++ b/solution.py
@@ -64,26 +64,35 @@
     )(value, *after)
 
 
+def in_hbm(value):
+    return pltpu.with_memory_space_constraint(value, pltpu.HBM)
+
+
 def row_of(place, h, slot, j):
     x, c = place[0], place[2]
     core = c if slot == 0 else 1 - c
     return pl.multiple_of(lax.rem(x + j, NX) * (4 * PIECE) + h * (2 * PIECE) + core * PIECE, 32)
 
 
-def prepare_kernel(place, act, cot, live, master, bias, mine, lead, own, shard, flipped, ordered):
+def prepare_kernel(place, act, cot, live, master, bias, mine, lead, own, shard, act_here, cot_here, flipped, ordered, sems):
+    loads = [pltpu.make_async_copy(act, act_here, sems.at[0]), pltpu.make_async_copy(cot, cot_here, sems.at[1])]
+    for load in loads:
+        load.start()
+    loads[0].wait()
     h = place[1]
-    flipped[...] = act[...].T
+    flipped[...] = act_here[...].T
     for slot in range(2):
         for j in range(NX):
             start = slot * HALF + j * PIECE
             ordered[pl.ds(start, PIECE), :] = flipped[pl.ds(row_of(place, 1 - h, slot, j), PIECE), :]
             start += 2 * HALF
             ordered[pl.ds(start, PIECE), :] = flipped[pl.ds(row_of(place, h, slot, j), PIECE), :]
-    wide = cot.shape[1]
+    wide = cot_here.shape[1]
     lead[:, wide:] = ordered[: 2 * HALF, :].T
     own[...] = ordered[2 * HALF : 3 * HALF, :].T
     mine[:, wide:] = ordered[3 * HALF :, :].T
-    masked = jnp.where(live[...] >= 0, cot[...], jnp.zeros((), bf16))
+    loads[1].wait()
+    masked = jnp.where(live[...] >= 0, cot_here[...], jnp.zeros((), bf16))
     lead[:, :wide] = masked
     mine[:, :wide] = masked
     shard[...] = master[...].astype(bf16)
@@ -95,12 +104,18 @@
     return pl.pallas_call(
         prepare_kernel,
         out_shape=[jax.ShapeDtypeStruct(shape, bf16) for shape in shapes],
-        in_specs=[SMEM, VMEM, VMEM, VMEM, VMEM, SMEM],
+        in_specs=[SMEM, ANY, ANY, VMEM, VMEM, SMEM],
         out_specs=[VMEM] * 4,
-        scratch_shapes=[pltpu.VMEM((wide, rows), bf16), pltpu.VMEM((wide, rows), bf16)],
-        compiler_params=room(14),
+        scratch_shapes=[
+            pltpu.VMEM((rows, wide), bf16),
+            pltpu.VMEM((rows, wide), bf16),
+            pltpu.VMEM((wide, rows), bf16),
+            pltpu.VMEM((wide, rows), bf16),
+            pltpu.SemaphoreType.DMA((2,)),
+        ],
+        compiler_params=room(18),
         cost_estimate=cost(0, 8 * rows * wide),
-    )(place, activations, cotangent, token_ids[:, None], master, bias)
+    )(place, in_hbm(activations), in_hbm(cotangent), token_ids[:, None], master, bias)
 
 
 OVER_ROWS = (((0,), (0,)), ((), ()))
@@ -276,23 +291,38 @@
     )(bias, master, first, second, here, *low, *high)
 
 
-def finish_kernel(place, ours, theirs, base, arrived, stepped, other, output, act_grad, averaged, ordered):
+def finish_kernel(place, ours, base, theirs, arrived, stepped, other, output, act_grad, averaged, *scratch):
+    ordered, ours_here, base_here, sems = scratch
     h = place[1]
     step = pl.program_id(0)
+    steps, _, width = base_here.shape
+    loads = [
+        pltpu.make_async_copy(base.at[:, i * width : (i + 1) * width], base_here.at[i], sems.at[i])
+        for i in range(steps)
+    ]
 
     @pl.when(step == 0)
     def _():
+        load = pltpu.make_async_copy(ours, ours_here, sems.at[steps])
+        load.start()
+        for part in loads:
+            part.start()
+        load.wait()
         for slot in range(2):
             for j in range(NX):
                 start = slot * HALF + j * PIECE
                 piece = slice(start, start + PIECE)
-                ordered[pl.ds(row_of(place, h, slot, j), PIECE), :] = ours[piece, :]
+                ordered[pl.ds(row_of(place, h, slot, j), PIECE), :] = ours_here[piece, :]
                 ordered[pl.ds(row_of(place, 1 - h, slot, j), PIECE), :] = theirs[piece, :]
 
-    width = act_grad.shape[1]
     act_grad[...] = ordered[pl.ds(pl.multiple_of(step * width, width), width), :].T
-    output[...] = (base[...] + arrived[...].astype(f32)).astype(bf16)
     averaged[...] = 0.5 * (stepped[...] + other[...].astype(f32))
+    for i in range(steps):
+
+        @pl.when(step == i)
+        def _():
+            loads[i].wait()
+            output[...] = (base_here[i] + arrived[...].astype(f32)).astype(bf16)
 
 
 def finish(place, ours, theirs, base, arrived, stepped, other):
@@ -311,12 +341,17 @@
             jax.ShapeDtypeStruct((rows, 2 * depth), bf16),
             jax.ShapeDtypeStruct((mine, wide), f32),
         ],
-        in_specs=[SMEM, whole, whole, cols, cols, part, part],
+        in_specs=[SMEM, ANY, ANY, whole, cols, part, part],
         out_specs=[cols, cols, part],
-        scratch_shapes=[pltpu.VMEM((2 * depth, rows), bf16)],
-        compiler_params=room(14),
+        scratch_shapes=[
+            pltpu.VMEM((2 * depth, rows), bf16),
+            pltpu.VMEM((depth, rows), bf16),
+            pltpu.VMEM((steps, rows, wide // steps), f32),
+            pltpu.SemaphoreType.DMA((steps + 1,)),
+        ],
+        compiler_params=room(18),
         cost_estimate=cost(4 * rows * wide, 18 * rows * wide),
-    )(place, ours, theirs, base, arrived, stepped, other)
+    )(place, in_hbm(ours), in_hbm(base), theirs, arrived, stepped, other)
 
 
 def from_partner(value, bit_index):

time: 151 us -> 150 us (level); the launches traced: 152 us -> 150 us
  local copies, waits for them, and re-layouts: 18.4 us -> 12.9 us
  Pallas kernels: 28.2 us -> 30.7 us
    unnamed x56 -> x48, local copies, waits for them, and re-layouts: 17.6 us -> 12.1 us
where the time goes in v1:
time: 150 us
  waiting for transfers between devices  80.1 us (53%)
  Pallas kernels  30.7 us (20%)
  starting transfers between devices  24 us (16%)
  local copies, waits for them, and re-layouts  12.9 us (9%)
  between operations  1.79 us (1%)
    ppermute x18, waiting for transfers between devices, send(): return lax.ppermute(value, 'fsdp', pairs)  60.1 us
    ppermute x18, starting transfers between devices, send(): return lax.ppermute(value, 'fsdp', pairs)  20.9 us
    ppermute x1, waiting for transfers between devices, from_partner(): return lax.ppermute(value, 'group', pairs)  20 us
    unnamed x48, local copies, waits for them, and re-layouts  12.1 us
    pallas_call x1, Pallas kernels, finish(): pl.pallas_call(finish_kernel, grid=(steps,), out_shape=[jax.ShapeDtypeStr...  6.88 us
    pallas_call x1, Pallas kernels, products(): pl.pallas_call(partial(products_kernel, len(weights)), out_shape=[jax.Sha...  6.48 us
    pallas_call x1, Pallas kernels, adam(): pl.pallas_call(adam_kernel, grid=(steps,), out_shape=[jax.ShapeDtypeStruc...  4.95 us
    pallas_call x1, Pallas kernels, gradient_blocks(): pl.pallas_call(gradient_kernel, out_shape=[jax.ShapeDtypeStruct((PIECE, w...  4.42 us
  transfers between devices with their start and end apart: 19, of which 7 were waited for; matrix products, arithmetic and copies ran while one was open for 0% of the time, Pallas kernels for 14%

profile of v1, /device:TPU:1, one launch (start us, length us, event | category | flops | bytes accessed | tf_op | source)
XLA Modules:
  0.0 149.7 jit_solution(14859527383921054984)
XLA Ops:
  2.4 1.4 copy-done.6
  3.8 3.0 %shard_map.110 = (bf16[256,3200]{1,0:T(8,128)(2,1)S(1)}, bf16[256,3840]{1,0:T(8,128)(2,1)S(1)}, bf16[256,640]{1,0:T(8,128)(2,1)S(1)}, bf16[160,2560]{1,0:T(8,128)(2,1)S(1)}) custom-call(s32[3]{0:T(128)S(1)} %pad_add_fusion.place, bf16[256,2560]{1,0:T(8,128)(2,1)} %act.1, bf16[256,2560]{1,0:T(8,128)(2,1)} %cot.1, s32[256,1]{1,0:T(8,128)S(1)} %copy.13.live, ...), custom_call_target="tpu_custom_call" | custom-call | flops 1 | bytes 1 | tf_op jit(solution)/shard_map/pallas_call | solution.py:104
  6.9 3.3 %collective-permute-start.9 = (bf16[160,2560]{1,0:T(8,128)(2,1)S(1)}, bf16[160,2560]{1,0:T(8,128)(2,1)S(1)}, u32[]{:S(2)}, u32[]{:S(2)}) collective-permute-start(bf16[160,2560]{1,0:T(8,128)(2,1)S(1)} %get-tuple-element.56.refs_0_), channel_id=1, source_target_pairs={{0,1},{1,0},{2,3},{3,2},{4,5},{5,4},{6,7},{7,6},{8,9},{9,8},{10,11... | collective-permute-start | bytes 2457608 | tf_op jit(solution)/shard_map/ppermute | solution.py:48
  11.4 2.5 %collective-permute-start.10 = (bf16[160,2560]{1,0:T(8,128)(2,1)S(1)}, bf16[160,2560]{1,0:T(8,128)(2,1)S(1)}, u32[]{:S(2)}, u32[]{:S(2)}) collective-permute-start(bf16[160,2560]{1,0:T(8,128)(2,1)S(1)} %get-tuple-element.56.refs_0_), channel_id=1, source_target_pairs={{0,12},{1,13},{2,14},{3,15},{4,0},{5,1},{6,2},{7,3},{8,4},{9,5},{1... | collective-permute-start | bytes 2457608 | tf_op jit(solution)/shard_map/ppermute | solution.py:48
  15.0 1.2 collective-permute-start.16
  16.2 32.3 %collective-permute-done.10.refs_1_ = bf16[160,2560]{1,0:T(8,128)(2,1)S(1)} collective-permute-done((bf16[160,2560]{1,0:T(8,128)(2,1)S(1)}, bf16[160,2560]{1,0:T(8,128)(2,1)S(1)}, u32[]{:S(2)}, u32[]{:S(2)}) %collective-permute-start.10) | collective-permute-done | bytes 819232 | tf_op jit(solution)/shard_map/ppermute | solution.py:48
  48.5 1.4 collective-permute-start.11
  50.0 3.1 %collective-permute-done.14.refs_3_ = bf16[160,2560]{1,0:T(8,128)(2,1)S(1)} collective-permute-done((bf16[160,2560]{1,0:T(8,128)(2,1)S(1)}, bf16[160,2560]{1,0:T(8,128)(2,1)S(1)}, u32[]{:S(2)}, u32[]{:S(2)}) %collective-permute-start.14) | collective-permute-done | bytes 819232 | tf_op jit(solution)/shard_map/ppermute | solution.py:48
  53.6 1.9 %collective-permute-done.15.refs_4_.refs_7_ = bf16[160,2560]{1,0:T(8,128)(2,1)S(1)} collective-permute-done((bf16[160,2560]{1,0:T(8,128)(2,1)S(1)}, bf16[160,2560]{1,0:T(8,128)(2,1)S(1)}, u32[]{:S(2)}, u32[]{:S(2)}) %collective-permute-start.15) | collective-permute-done | bytes 819232 | tf_op jit(solution)/shard_map/ppermute | solution.py:48
  57.0 4.0 %shard_map.112.refs_0_ = bf16[256,2560]{1,0:T(8,128)(2,1)} custom-call(bf16[256,3840]{1,0:T(8,128)(2,1)S(1)} %shard_map.111.lead, bf16[160,2560]{1,0:T(8,128)(2,1)S(1)} %get-tuple-element.56.refs_0_, bf16[160,2560]{1,0:T(8,128)(2,1)S(1)} %collective-permute-done.10.refs_1_, bf16[160,2560]{1,0:T(8,128)(2,1)S(1)} %collective-permute-done.12.refs_2_, ...), custom_call_target="tpu_custom_call" | custom-call | flops 1 | bytes 1 | tf_op jit(solution)/shard_map/pallas_call | solution.py:205
  62.2 4.4 %shard_map.113 = (f32[160,2560]{1,0:T(8,128)S(1)}, bf16[80,2560]{1,0:T(8,128)(2,1)S(1)}, bf16[80,2560]{1,0:T(8,128)(2,1)}, bf16[80,2560]{1,0:T(8,128)(2,1)S(1)},...) custom-call(bf16[256,640]{1,0:T(8,128)(2,1)S(1)} %get-tuple-element.57.own, ...), custom_call_target="tpu_custom_call" | custom-call | flops 1 | bytes 1 | tf_op jit(solution)/shard_map/pallas_call | solution.py:146
  67.8 1.2 collective-permute-start.18
  69.0 1.5 collective-permute-start.19
  70.5 1.3 collective-permute-start.21
  71.9 7.9 %collective-permute-done.18.refs_2_ = bf16[80,2560]{1,0:T(8,128)(2,1)S(1)} collective-permute-done((bf16[80,2560]{1,0:T(8,128)(2,1)S(1)}, bf16[80,2560]{1,0:T(8,128)(2,1)S(1)}, u32[]{:S(2)}, u32[]{:S(2)}) %collective-permute-start.18) | collective-permute-done | bytes 409632 | tf_op jit(solution)/shard_map/ppermute | solution.py:48
  81.8 1.8 %collective-permute-start.23 = (bf16[80,2560]{1,0:T(8,128)(2,1)}, bf16[80,2560]{1,0:T(8,128)(2,1)}, u32[]{:S(2)}, u32[]{:S(2)}) collective-permute-start(bf16[80,2560]{1,0:T(8,128)(2,1)} %get-tuple-element.68), channel_id=1, source_target_pairs={{0,12},{1,13},{2,14},{3,15},{4,0},{5,1},{6,2},{7,3},{8,4},{9,5},{1... | collective-permute-start | bytes 1228808 | tf_op jit(solution)/shard_map/ppermute | solution.py:48
  87.0 1.4 copy-done.9
  93.0 6.5 %shard_map.115 = (bf16[1280,256]{1,0:T(8,128)(2,1)S(1)}, bf16[1280,256]{1,0:T(8,128)(2,1)S(1)}, f32[256,2560]{1,0:T(8,128)S(1)}) custom-call(bf16[256,3200]{1,0:T(8,128)(2,1)S(1)} %copy-done.9, bf16[256,3840]{1,0:T(8,128)(2,1)S(1)} %shard_map.111.lead, bf16[256,640]{1,0:T(8,128)(2,1)S(1)} %get-tuple-element.57.own, bf16[160,2560]{1,0:T(8,128)(2,1)S(1)} %copy-done.11, ...), custom_call_target="tpu_custom_call" | custom-call | flops 1 | bytes 1 | tf_op jit(solution)/shard_map/pallas_call | solution.py:235
  99.6 4.9 %shard_map.116 = (f32[160,2560]{1,0:T(8,128)S(1)}, bf16[160,2560]{1,0:T(8,128)(2,1)S(1)}, bf16[160,2560]{1,0:T(8,128)(2,1)}, bf16[160,2560]{1,0:T(8,128)(2,1)}) custom-call(f32[2]{0:T(128)S(1)} %pad_maximum_fusion.bias, f32[160,2560]{1,0:T(8,128)S(1)} %bitcast.18, bf16[160,2560]{1,0:T(8,128)(2,1)S(1)} %bitcast.19, bf16[160,2560]{1,0:T(8,128)(2,1)S(1)} %bitcast.20, ...), custom_call_target="tpu_custom_call" | custom-call | flops 1 | bytes 1 | tf_op jit(solution)/shard_map/pallas_call | solution.py:283
  104.6 38.0 %conditional.1 = (bf16[160,2560]{1,0:T(8,128)(2,1)}, bf16[1280,256]{1,0:T(8,128)(2,1)}) conditional(s32[]{:T(128)} %clamp.3, (bf16[160,2560]{1,0:T(8,128)(2,1)S(1)}, bf16[1280,256]{1,0:T(8,128)(2,1)S(1)}) %tuple.24, (bf16[160,2560]{1,0:T(8,128)(2,1)S(1)}, bf16[1280,256]{1,0:T(8,128)(2,1)S(1)}) %tuple.24, ...), branch_computations={%region_0.1_spmd, %region_1.2_spmd, %region_2.3_spmd, %region_3.4_... | conditional | bytes 5898336 | solution.py:370
  104.6 3.1 %collective-permute-start.2 = (bf16[160,2560]{1,0:T(8,128)(2,1)S(1)}, bf16[160,2560]{1,0:T(8,128)(2,1)}, u32[]{:S(2)}, u32[]{:S(2)}) collective-permute-start(bf16[160,2560]{1,0:T(8,128)(2,1)S(1)} %get-tuple-element.18), channel_id=1, source_target_pairs={{0,32},{16,48},{32,0},{48,16},{64,96},{80,112},{96,64},{112,80},{1... | collective-permute-start | bytes 2457608 | tf_op jit(solution)/shard_map/cond/branch_1_fun/ppermute | solution.py:360
  108.4 14.2 %collective-permute-done.3 = bf16[1280,256]{1,0:T(8,128)(2,1)} collective-permute-done((bf16[1280,256]{1,0:T(8,128)(2,1)S(1)}, bf16[1280,256]{1,0:T(8,128)(2,1)}, u32[]{:S(2)}, u32[]{:S(2)}) %collective-permute-start.3) | collective-permute-done | bytes 655392 | tf_op jit(solution)/shard_map/cond/branch_1_fun/ppermute | solution.py:48
  122.6 20.0 %collective-permute-done.2 = bf16[160,2560]{1,0:T(8,128)(2,1)} collective-permute-done((bf16[160,2560]{1,0:T(8,128)(2,1)S(1)}, bf16[160,2560]{1,0:T(8,128)(2,1)}, u32[]{:S(2)}, u32[]{:S(2)}) %collective-permute-start.2) | collective-permute-done | bytes 819232 | tf_op jit(solution)/shard_map/cond/branch_1_fun/ppermute | solution.py:360
  142.6 6.9 %shard_map.117 = (bf16[256,2560]{1,0:T(8,128)(2,1)}, bf16[256,2560]{1,0:T(8,128)(2,1)}, f32[160,2560]{1,0:T(8,128)}) custom-call(s32[3]{0:T(128)S(1)} %pad_add_fusion.place, bf16[1280,256]{1,0:T(8,128)(2,1)} %copy-done.23, f32[256,2560]{1,0:T(8,128)} %copy-done.18, bf16[1280,256]{1,0:T(8,128)(2,1)} %get-tuple-element.71.theirs, ...), custom_call_target="tpu_custom_call" | custom-call | flops 1 | bytes 1 | tf_op jit(solution)/shard_map/pallas_call | solution.py:336
  (74 shorter events, 18.6 us)
Async XLA Ops:
  6.8 50.1 %copy-start.10 = (bf16[160,2560]{1,0:T(8,128)(2,1)}, bf16[160,2560]{1,0:T(8,128)(2,1)S(1)}, u32[]{:S(2)}) copy-start(bf16[160,2560]{1,0:T(8,128)(2,1)S(1)} %get-tuple-element.56.refs_0_) | copy-start | bytes 2457604
  6.8 55.3 %copy-start.8 = (bf16[256,3200]{1,0:T(8,128)(2,1)}, bf16[256,3200]{1,0:T(8,128)(2,1)S(1)}, u32[]{:S(2)}) copy-start(bf16[256,3200]{1,0:T(8,128)(2,1)S(1)} %get-tuple-element.54.mine) | copy-start | bytes 4915204
  6.9 8.1 %collective-permute-start.9 = (bf16[160,2560]{1,0:T(8,128)(2,1)S(1)}, bf16[160,2560]{1,0:T(8,128)(2,1)S(1)}, u32[]{:S(2)}, u32[]{:S(2)}) collective-permute-start(bf16[160,2560]{1,0:T(8,128)(2,1)S(1)} %get-tuple-element.56.refs_0_), channel_id=1, source_target_pairs={{0,1},{1,0},{2,3},{3,2},{4,5},{5,4},{6,7},{7,6},{8,9},{9,8},{10,11... | collective-permute-start | bytes 2457608 | tf_op jit(solution)/shard_map/ppermute | solution.py:48
  10.2 45.9 %collective-permute-start.8 = (bf16[256,3840]{1,0:T(8,128)(2,1)S(1)}, bf16[256,3840]{1,0:T(8,128)(2,1)S(1)}, u32[]{:S(2)}, u32[]{:S(2)}) collective-permute-start(bf16[256,3840]{1,0:T(8,128)(2,1)S(1)} %get-tuple-element.55), channel_id=1, source_target_pairs={{0,2},{1,3},{2,0},{3,1},{4,6},{5,7},{6,4},{7,5},{8,10},{9,11},{10,... | collective-permute-start | bytes 5898248 | tf_op jit(solution)/shard_map/ppermute | solution.py:48
  11.4 37.2 %collective-permute-start.10 = (bf16[160,2560]{1,0:T(8,128)(2,1)S(1)}, bf16[160,2560]{1,0:T(8,128)(2,1)S(1)}, u32[]{:S(2)}, u32[]{:S(2)}) collective-permute-start(bf16[160,2560]{1,0:T(8,128)(2,1)S(1)} %get-tuple-element.56.refs_0_), channel_id=1, source_target_pairs={{0,12},{1,13},{2,14},{3,15},{4,0},{5,1},{6,2},{7,3},{8,4},{9,5},{1... | collective-permute-start | bytes 2457608 | tf_op jit(solution)/shard_map/ppermute | solution.py:48
  13.9 36.1 %collective-permute-start.12 = (bf16[160,2560]{1,0:T(8,128)(2,1)S(1)}, bf16[160,2560]{1,0:T(8,128)(2,1)S(1)}, u32[]{:S(2)}, u32[]{:S(2)}) collective-permute-start(bf16[160,2560]{1,0:T(8,128)(2,1)S(1)} %get-tuple-element.56.refs_0_), channel_id=1, source_target_pairs={{0,8},{1,9},{2,10},{3,11},{4,12},{5,13},{6,14},{7,15},{8,0},{9,1},... | collective-permute-start | bytes 2457608 | tf_op jit(solution)/shard_map/ppermute | solution.py:48
  14.4 38.7 %collective-permute-start.14 = (bf16[160,2560]{1,0:T(8,128)(2,1)S(1)}, bf16[160,2560]{1,0:T(8,128)(2,1)S(1)}, u32[]{:S(2)}, u32[]{:S(2)}) collective-permute-start(bf16[160,2560]{1,0:T(8,128)(2,1)S(1)} %get-tuple-element.56.refs_0_), channel_id=1, source_target_pairs={{0,4},{1,5},{2,6},{3,7},{4,8},{5,9},{6,10},{7,11},{8,12},{9,13},{1... | collective-permute-start | bytes 2457608 | tf_op jit(solution)/shard_map/ppermute | solution.py:48
  15.0 40.6 %collective-permute-start.16 = (bf16[256,3200]{1,0:T(8,128)(2,1)S(1)}, bf16[256,3200]{1,0:T(8,128)(2,1)S(1)}, u32[]{:S(2)}, u32[]{:S(2)}) collective-permute-start(bf16[256,3200]{1,0:T(8,128)(2,1)S(1)} %get-tuple-element.54.mine), channel_id=1, source_target_pairs={{0,1},{1,0},{2,3},{3,2},{4,5},{5,4},{6,7},{7,6},{8,9},{9,8},{10,11... | collective-permute-start | bytes 4915208 | tf_op jit(solution)/shard_map/ppermute | solution.py:48
  48.5 8.4 %copy-start.12 = (bf16[160,2560]{1,0:T(8,128)(2,1)}, bf16[160,2560]{1,0:T(8,128)(2,1)S(1)}, u32[]{:S(2)}) copy-start(bf16[160,2560]{1,0:T(8,128)(2,1)S(1)} %collective-permute-done.10.refs_1_) | copy-start | bytes 2457604
  48.5 5.0 %collective-permute-start.11 = (bf16[160,2560]{1,0:T(8,128)(2,1)S(1)}, bf16[160,2560]{1,0:T(8,128)(2,1)S(1)}, u32[]{:S(2)}, u32[]{:S(2)}) collective-permute-start(bf16[160,2560]{1,0:T(8,128)(2,1)S(1)} %collective-permute-done.10.refs_1_), channel_id=1, source_target_pairs={{0,1},{1,0},{2,3},{3,2},{4,5},{5,4},{6,7},{7,6},{8,9},{9,8},{10,11... | collective-permute-start | bytes 2457608 | tf_op jit(solution)/shard_map/ppermute | solution.py:48
  49.9 7.0 %copy-start.14 = (bf16[160,2560]{1,0:T(8,128)(2,1)}, bf16[160,2560]{1,0:T(8,128)(2,1)S(1)}, u32[]{:S(2)}) copy-start(bf16[160,2560]{1,0:T(8,128)(2,1)S(1)} %collective-permute-done.12.refs_2_) | copy-start | bytes 2457604
  49.9 3.7 %collective-permute-start.13 = (bf16[160,2560]{1,0:T(8,128)(2,1)S(1)}, bf16[160,2560]{1,0:T(8,128)(2,1)S(1)}, u32[]{:S(2)}, u32[]{:S(2)}) collective-permute-start(bf16[160,2560]{1,0:T(8,128)(2,1)S(1)} %collective-permute-done.12.refs_2_), channel_id=1, source_target_pairs={{0,1},{1,0},{2,3},{3,2},{4,5},{5,4},{6,7},{7,6},{8,9},{9,8},{10,11... | collective-permute-start | bytes 2457608 | tf_op jit(solution)/shard_map/ppermute | solution.py:48
  53.1 2.5 %collective-permute-start.15 = (bf16[160,2560]{1,0:T(8,128)(2,1)S(1)}, bf16[160,2560]{1,0:T(8,128)(2,1)S(1)}, u32[]{:S(2)}, u32[]{:S(2)}) collective-permute-start(bf16[160,2560]{1,0:T(8,128)(2,1)S(1)} %collective-permute-done.14.refs_3_), channel_id=1, source_target_pairs={{0,1},{1,0},{2,3},{3,2},{4,5},{5,4},{6,7},{7,6},{8,9},{9,8},{10,11... | collective-permute-start | bytes 2457608 | tf_op jit(solution)/shard_map/ppermute | solution.py:48
  56.1 6.1 %collective-permute-start.17 = (bf16[256,3840]{1,0:T(8,128)(2,1)S(1)}, bf16[256,3840]{1,0:T(8,128)(2,1)S(1)}, u32[]{:S(2)}, u32[]{:S(2)}) collective-permute-start(bf16[256,3840]{1,0:T(8,128)(2,1)S(1)} %shard_map.111.lead), channel_id=1, source_target_pairs={{0,1},{1,0},{2,3},{3,2},{4,5},{5,4},{6,7},{7,6},{8,9},{9,8},{10,11... | collective-permute-start | bytes 5898248 | tf_op jit(solution)/shard_map/ppermute | solution.py:48
  61.0 81.6 %collective-permute-start.24 = (bf16[256,2560]{1,0:T(8,128)(2,1)}, bf16[256,2560]{1,0:T(8,128)(2,1)}, u32[]{:S(2)}, u32[]{:S(2)}) collective-permute-start(bf16[256,2560]{1,0:T(8,128)(2,1)} %shard_map.112.refs_0_), channel_id=1, source_target_pairs={{0,2},{1,3},{2,0},{3,1},{4,6},{5,7},{6,4},{7,5},{8,10},{9,11},{10,... | collective-permute-start | bytes 3932168 | tf_op jit(solution)/shard_map/ppermute | solution.py:48
  67.8 12.1 %collective-permute-start.18 = (bf16[80,2560]{1,0:T(8,128)(2,1)S(1)}, bf16[80,2560]{1,0:T(8,128)(2,1)S(1)}, u32[]{:S(2)}, u32[]{:S(2)}) collective-permute-start(bf16[80,2560]{1,0:T(8,128)(2,1)S(1)} %get-tuple-element.60), channel_id=1, source_target_pairs={{0,4},{1,5},{2,6},{3,7},{4,8},{5,9},{6,10},{7,11},{8,12},{9,13},{1... | collective-permute-start | bytes 1228808 | tf_op jit(solution)/shard_map/ppermute | solution.py:48
  69.0 10.9 %collective-permute-start.19 = (bf16[80,2560]{1,0:T(8,128)(2,1)S(1)}, bf16[80,2560]{1,0:T(8,128)(2,1)S(1)}, u32[]{:S(2)}, u32[]{:S(2)}) collective-permute-start(bf16[80,2560]{1,0:T(8,128)(2,1)S(1)} %get-tuple-element.61), channel_id=1, source_target_pairs={{0,12},{1,13},{2,14},{3,15},{4,0},{5,1},{6,2},{7,3},{8,4},{9,5},{1... | collective-permute-start | bytes 1228808 | tf_op jit(solution)/shard_map/ppermute | solution.py:48
  70.5 29.1 %collective-permute-start.21 = (bf16[80,2560]{1,0:T(8,128)(2,1)}, bf16[80,2560]{1,0:T(8,128)(2,1)S(1)}, u32[]{:S(2)}, u32[]{:S(2)}) collective-permute-start(bf16[80,2560]{1,0:T(8,128)(2,1)} %get-tuple-element.66), channel_id=1, source_target_pairs={{0,12},{1,13},{2,14},{3,15},{4,0},{5,1},{6,2},{7,3},{8,4},{9,5},{1... | collective-permute-start | bytes 1228808 | tf_op jit(solution)/shard_map/ppermute | solution.py:48
  71.7 27.8 %collective-permute-start.22 = (bf16[80,2560]{1,0:T(8,128)(2,1)}, bf16[80,2560]{1,0:T(8,128)(2,1)}, u32[]{:S(2)}, u32[]{:S(2)}) collective-permute-start(bf16[80,2560]{1,0:T(8,128)(2,1)} %get-tuple-element.67), channel_id=1, source_target_pairs={{0,4},{1,5},{2,6},{3,7},{4,8},{5,9},{6,10},{7,11},{8,12},{9,13},{1... | collective-permute-start | bytes 1228808 | tf_op jit(solution)/shard_map/ppermute | solution.py:48
  80.9 18.7 %collective-permute-start.20 = (bf16[80,2560]{1,0:T(8,128)(2,1)}, bf16[80,2560]{1,0:T(8,128)(2,1)}, u32[]{:S(2)}, u32[]{:S(2)}) collective-permute-start(bf16[80,2560]{1,0:T(8,128)(2,1)} %get-tuple-element.62.refs_8_), channel_id=1, source_target_pairs={{0,4},{1,5},{2,6},{3,7},{4,8},{5,9},{6,10},{7,11},{8,12},{9,13},{1... | collective-permute-start | bytes 1228808 | tf_op jit(solution)/shard_map/ppermute | solution.py:48
  81.8 17.8 %collective-permute-start.23 = (bf16[80,2560]{1,0:T(8,128)(2,1)}, bf16[80,2560]{1,0:T(8,128)(2,1)}, u32[]{:S(2)}, u32[]{:S(2)}) collective-permute-start(bf16[80,2560]{1,0:T(8,128)(2,1)} %get-tuple-element.68), channel_id=1, source_target_pairs={{0,12},{1,13},{2,14},{3,15},{4,0},{5,1},{6,2},{7,3},{8,4},{9,5},{1... | collective-permute-start | bytes 1228808 | tf_op jit(solution)/shard_map/ppermute | solution.py:48
  93.0 6.6 %copy-start.22 = (bf16[1,160,2560]{2,1,0:T(8,128)(2,1)S(1)}, bf16[1,160,2560]{2,1,0:T(8,128)(2,1)}, u32[]{:S(2)}) copy-start(bf16[1,160,2560]{2,1,0:T(8,128)(2,1)} %param.17) | copy-start | bytes 2457604
  104.6 38.0 %collective-permute-start.2 = (bf16[160,2560]{1,0:T(8,128)(2,1)S(1)}, bf16[160,2560]{1,0:T(8,128)(2,1)}, u32[]{:S(2)}, u32[]{:S(2)}) collective-permute-start(bf16[160,2560]{1,0:T(8,128)(2,1)S(1)} %get-tuple-element.18), channel_id=1, source_target_pairs={{0,32},{16,48},{32,0},{48,16},{64,96},{80,112},{96,64},{112,80},{1... | collective-permute-start | bytes 2457608 | tf_op jit(solution)/shard_map/cond/branch_1_fun/ppermute | solution.py:360
  107.7 14.9 %collective-permute-start.3 = (bf16[1280,256]{1,0:T(8,128)(2,1)S(1)}, bf16[1280,256]{1,0:T(8,128)(2,1)}, u32[]{:S(2)}, u32[]{:S(2)}) collective-permute-start(bf16[1280,256]{1,0:T(8,128)(2,1)S(1)} %get-tuple-element.19), channel_id=1, source_target_pairs={{0,2},{1,3},{2,0},{3,1},{4,6},{5,7},{6,4},{7,5},{8,10},{9,11},{10,... | collective-permute-start | bytes 1966088 | tf_op jit(solution)/shard_map/cond/branch_1_fun/ppermute | solution.py:48
  (19 other events, 53.9 us)
